TPU v7x, 32 devices: a whole 2x2x4 slice. The times are simulated.
32 devices in a mesh: dp: 8 (over z, x), tensor: 4 (over y, core).
Axes of the slice: x: 2, y: 2, z: 4, core: 2. Of those that a mesh axis runs over, the one named last changes fastest.
Arguments:
- gradient: bfloat16 [8, 512, 16384], P(None, 'dp', 'tensor')
- second_moment: bfloat16 [8, 512, 16384], P(None, 'dp', 'tensor'), may hold values from 0.049804688 to 2
- slot_of_block: int32 [4, 64], P('tensor'), may hold values from 0 to 127, as said below
- stats_left: float32 [4, 128, 512, 512], P('tensor', 'dp'), as said below
- stats_right: float32 [4, 128, 512, 512], P('tensor', 'dp'), as said below
- root_left: bfloat16 [4, 128, 512, 512], P('tensor', 'dp'), as said below
- root_right: bfloat16 [4, 128, 512, 512], P('tensor', 'dp'), as said below
Outputs:
- update: bfloat16 [8, 512, 16384], P(None, 'dp', 'tensor')
- second_moment_new: bfloat16 [8, 512, 16384], P(None, 'dp', 'tensor')
- stats_left_new: float32 [4, 128, 512, 512], P('tensor', 'dp')
- stats_right_new: float32 [4, 128, 512, 512], P('tensor', 'dp')
Inputs may be any that keep to these rules, and one draw needn't show every extreme that they name: `slot_of_block`: the entries of one row are distinct; slot s belongs to owner s // 16 of dp; in every row some owner holds 16 blocks. `stats_left`: symmetric matrices. `stats_right`: symmetric matrices. `root_left`: symmetric matrices. `root_right`: symmetric matrices.
All inputs are finite; a program needn't handle non-finite values.
Results may differ from a plain program's by a relative error of at most 0.0064.
Values may be sent and summed in bfloat16 or wider, within the bound.
A program may use at most 256 MiB of HBM per device.

v0:
```python
import math

import jax
import jax.numpy as jnp
from jax import lax
from jax.sharding import PartitionSpec as P

clip_level = 0.5
decay_moment = 0.95
decay_stats = 0.9
eps_adam = 1e-08
eps_graft = 1e-06


def per_device(
    gradient, second_moment, slot_of_block, stats_left, stats_right, root_left, root_right
):
    owners = lax.axis_size("dp")
    my_owner = lax.axis_index("dp")
    row_blocks, piece_rows, columns = gradient.shape
    block_size = piece_rows * owners
    col_blocks = columns // block_size
    block_count = row_blocks * col_blocks
    capacity = stats_left.shape[1]
    all_rows = row_blocks * block_size
    all_columns = columns * lax.axis_size("tensor")
    area = float(block_size * block_size)
    grad_wide = gradient.astype(jnp.float32)
    total_square = lax.psum(jnp.sum(grad_wide * grad_wide), ("dp", "tensor"))
    clip_factor = clip_level * math.sqrt(all_rows * all_columns) / jnp.sqrt(total_square)
    clipped = clip_factor * grad_wide
    moment = (
        decay_moment * second_moment.astype(jnp.float32) + (1.0 - decay_moment) * clipped * clipped
    )
    adam_step = clipped / (jnp.sqrt(moment) + eps_adam)
    moment_new = moment.astype(jnp.bfloat16)
    adam_part = jnp.sum(
        (adam_step * adam_step).reshape(row_blocks, piece_rows, col_blocks, block_size), axis=(1, 3)
    ).reshape(block_count)
    table = slot_of_block[0]
    slot_ids = jnp.arange(owners * capacity, dtype=jnp.int32)
    selector = (
        (table[None, :] == slot_ids[:, None])
        .astype(jnp.bfloat16)
        .reshape(owners * capacity, row_blocks, col_blocks)
    )
    grad_pieces = gradient.reshape(row_blocks, piece_rows, col_blocks, block_size)
    outgoing = jnp.einsum(
        "sij,irjb->srb", selector, grad_pieces, preferred_element_type=jnp.float32
    ).astype(jnp.bfloat16)
    arrived = lax.all_to_all(
        outgoing.reshape(owners, capacity, piece_rows, block_size),
        "dp",
        split_axis=0,
        concat_axis=2,
        tiled=True,
    )[0]
    my_slots = my_owner * capacity + jnp.arange(capacity, dtype=jnp.int32)
    owned = table[None, :] == my_slots[:, None]
    in_use = jnp.any(owned, axis=1)

    def compute(items):
        grad_block, left_old, right_old, root_one, root_two = items
        gram_left = lax.dot_general(
            grad_block, grad_block, (((1,), (1,)), ((), ())), preferred_element_type=jnp.float32
        )
        gram_right = lax.dot_general(
            grad_block, grad_block, (((0,), (0,)), ((), ())), preferred_element_type=jnp.float32
        )
        square_clip = clip_factor * clip_factor
        left_block = decay_stats * left_old + (1.0 - decay_stats) * square_clip * gram_left
        right_block = decay_stats * right_old + (1.0 - decay_stats) * square_clip * gram_right
        scaled = (clip_factor * grad_block.astype(jnp.float32)).astype(jnp.bfloat16)
        applied = jnp.dot(root_one, scaled, preferred_element_type=jnp.float32).astype(jnp.bfloat16)
        precond_block = jnp.dot(applied, root_two, preferred_element_type=jnp.float32).astype(
            jnp.bfloat16
        )
        return (left_block, right_block, precond_block)

    def keep(items):
        return (items[1], items[2], jnp.zeros_like(items[0]))

    def process(operands):
        grad_block, left_old, right_old, root_one, root_two, active = operands
        return lax.cond(
            active, compute, keep, (grad_block, left_old, right_old, root_one, root_two)
        )

    left_new, right_new, precond = lax.map(
        process, (arrived, stats_left[0], stats_right[0], root_left[0], root_right[0], in_use)
    )
    returned = lax.all_to_all(precond[None], "dp", split_axis=2, concat_axis=0, tiled=True)
    placed = jnp.einsum(
        "sij,srb->irjb",
        selector,
        returned.reshape(owners * capacity, piece_rows, block_size),
        preferred_element_type=jnp.float32,
    )
    precond_part = jnp.sum(placed * placed, axis=(1, 3)).reshape(block_count)
    adam_total, precond_total = lax.psum((adam_part, precond_part), "dp")
    ratio = jnp.sqrt(adam_total / area / (precond_total / area + eps_graft)).reshape(
        row_blocks, 1, col_blocks, 1
    )
    update = (ratio * placed).astype(jnp.bfloat16)
    return (
        update.reshape(row_blocks, piece_rows, columns),
        moment_new,
        left_new[None],
        right_new[None],
    )


def solution(mesh):
    placed = (
        P(None, "dp", "tensor"),
        P(None, "dp", "tensor"),
        P("tensor", None),
        P("tensor", "dp", None, None),
        P("tensor", "dp", None, None),
        P("tensor", "dp", None, None),
        P("tensor", "dp", None, None),
    )
    return jax.shard_map(
        per_device,
        mesh=mesh,
        in_specs=placed,
        out_specs=(
            P(None, "dp", "tensor"),
            P(None, "dp", "tensor"),
            P("tensor", "dp", None, None),
            P("tensor", "dp", None, None),
        ),
        check_vma=False,
    )
```

profile of v0, /device:TPU:12, one launch (start us, length us, event | category | flops | bytes accessed | tf_op | source)
XLA Modules:
  0.0 688.2 jit_solution(9934610879597102079)
XLA Ops:
  1.1 1.3 reduce.6
  2.5 4.4 copy.30
  7.0 6.1 bitcast_convert_fusion
  13.1 8.0 %copy.23 = bf16[8,16,64,512]{3,1,2,0:T(8,128)(2,1)} copy(bf16[8,16,64,512]{3,1,0,2:T(8,128)(2,1)} %bitcast.93) | data formatting | bytes 16777216 | tf_op jit(solution)/shard_map/reshape | solution.py:52
  21.1 6.4 all-to-all-start
  27.5 4.9 fusion.26
  32.4 197.3 %psum.21 = f32[]{:T(128)} all-reduce(f32[]{:T(128)} %fusion.26), channel_id=1, replica_groups=mesh['dp'=8,'tensor'=4] {'dp','tensor'}, use_global_device_ids=true, to_apply=%region_1.0 | all-reduce | flops 1 | bytes 8 | tf_op jit(solution)/shard_map/psum | solution.py:29
  230.6 11.3 %copy.24 = bf16[16,512,512]{2,1,0:T(8,128)(2,1)} copy(bf16[16,512,512]{2,0,1:T(8,128)(2,1)} %bitcast.21) | data formatting | bytes 16777216 | tf_op jit(solution)/shard_map/while | solution.py:89
  242.0 141.1 %while.14 = (s32[]{:T(128)}, f32[16,512,512]{2,1,0:T(8,128)}, f32[16,512,512]{2,1,0:T(8,128)}, bf16[16,512,512]{2,1,0:T(8,128)(2,1)}, pred[16]{0:T(512)(128)(4,1...) while((s32[]{:T(128)}, f32[16,512,512]{2,1,0:T(8,128)}, ...), condition=%wide.region_9.10_spmd, body=%wide.region_6.0_spmd.sunk | while | flops 1076625408 | bytes 16781576 | solution.py:89
  243.3 1.3 dynamic-slice_bitcast_fusion.5
  245.9 1.5 bitcast_dynamic-update-slice_fusion.3
  252.2 1.5 bitcast_dynamic-update-slice_fusion.3
  258.4 5.9 conditional.2
  258.4 1.8 fusion
  260.3 1.9 fusion.1
  262.2 2.1 fusion.2
  264.3 1.5 bitcast_dynamic-update-slice_fusion.3
  270.4 5.9 conditional.2
  270.5 1.9 fusion
  272.3 2.0 fusion.1
  274.3 2.1 fusion.2
  276.4 1.5 bitcast_dynamic-update-slice_fusion.3
  282.5 5.9 conditional.2
  282.6 1.8 fusion
  284.4 1.9 fusion.1
  286.3 2.1 fusion.2
  288.4 1.5 bitcast_dynamic-update-slice_fusion.3
  294.6 5.9 conditional.2
  294.7 1.9 fusion
  296.5 1.9 fusion.1
  298.5 2.1 fusion.2
  300.6 1.5 bitcast_dynamic-update-slice_fusion.3
  306.8 1.5 bitcast_dynamic-update-slice_fusion.3
  313.0 1.5 bitcast_dynamic-update-slice_fusion.3
  319.3 1.5 bitcast_dynamic-update-slice_fusion.3
  325.5 5.9 conditional.2
  325.5 1.8 fusion
  327.4 1.9 fusion.1
  329.3 2.1 fusion.2
  331.4 1.5 bitcast_dynamic-update-slice_fusion.3
  337.7 1.5 bitcast_dynamic-update-slice_fusion.3
  343.8 5.9 conditional.2
  343.8 1.9 fusion
  345.7 1.9 fusion.1
  347.7 2.1 fusion.2
  349.8 1.5 bitcast_dynamic-update-slice_fusion.3
  356.0 1.5 bitcast_dynamic-update-slice_fusion.3
  362.2 6.1 conditional.2
  362.2 2.0 fusion
  364.2 2.0 fusion.1
  366.2 2.1 fusion.2
  368.3 1.5 bitcast_dynamic-update-slice_fusion.3
  374.5 1.5 bitcast_dynamic-update-slice_fusion.3
  380.8 1.5 bitcast_dynamic-update-slice_fusion.3
  383.1 11.3 %copy.32 = bf16[16,512,512]{2,0,1:T(8,128)(2,1)} copy(bf16[16,512,512]{2,1,0:T(8,128)(2,1)} %get-tuple-element.139) | data formatting | bytes 16777216 | tf_op jit(solution)/shard_map/while | solution.py:89
  394.4 58.1 %all-to-all-start.1 = ((bf16[1,16,512,512]{3,1,0,2:T(8,128)(2,1)}), bf16[1,16,512,512]{3,1,0,2:T(8,128)(2,1)}, u32[]{:S(2)}, u32[]{:S(2)}) async-start(bf16[1,16,512,512]{3,1,0,2:T(8,128)(2,1)} %bitcast.92), calls=%async_computation.1 | async-start | bytes 16777216 | tf_op jit(solution)/shard_map/all_to_all | solution.py:92
  452.5 8.9 %fusion.29 = (bf16[8,64,4096]{2,1,0:T(8,128)(2,1)}, f32[8,4096]{1,0:T(8,128)S(1)}) fusion(bf16[8,64,4096]{2,1,0:T(8,128)(2,1)} %param.11, bf16[8,64,4096]{2,1,0:T(8,128)(2,1)} %param.12, f32[]{:T(128)} %div.15), kind=kLoop, calls=%fused_computation.39 | loop fusion | flops 25133056 | bytes 12713988 | tf_op jit(solution)/shard_map/convert_element_type | solution.py:36
  461.7 170.6 %all-to-all-done.1 = bf16[1,16,512,512]{3,1,0,2:T(8,128)(2,1)} async-done(((bf16[1,16,512,512]{3,1,0,2:T(8,128)(2,1)}), bf16[1,16,512,512]{3,1,0,2:T(8,128)(2,1)}, u32[]{:S(2)}, u32[]{:S(2)}) %all-to-all-start.1) | async-done | bytes 8388640 | tf_op jit(solution)/shard_map/all_to_all | solution.py:92
  632.3 8.0 %copy.26 = bf16[1,16,8,64,512]{4,1,2,3,0:T(8,128)(2,1)} copy(bf16[1,16,8,64,512]{4,1,3,2,0:T(8,128)(2,1)} %bitcast.25) | data formatting | bytes 16777216 | tf_op jit(solution)/shard_map/all_to_all | solution.py:92
  640.3 8.2 %multiply_reduce_fusion = (f32[8,8]{1,0:T(8,128)S(1)}, f32[64,512,8,8]{1,3,2,0:T(8,128)}) fusion(bf16[128,64,512,1]{2,0,3,1:T(8,128)(2,1)} %bitcast.90, s32[8,8]{1,0:T(8,128)S(1)} %eq.54), kind=kOutput, calls=%fused_computation.37 | convolution fusion | flops 541073344 | bytes 16777728 | tf_op jit(solution)/shard_map/sij,srb->irjb/dot_general | solution.py:93
  648.6 18.8 %all-reduce = (f32[64]{0:T(128)S(1)}, f32[64]{0:T(128)S(1)}) all-reduce(f32[64]{0:T(128)S(1)} %reshape.71, f32[64]{0:T(128)S(1)} %reshape.67), channel_id=1, replica_groups=mesh['dp'=8,'tensor'=4] {'dp'}, use_global_device_ids=true, to_apply=%region_11.12 | all-reduce | flops 128 | bytes 1024 | tf_op jit(solution)/shard_map/psum | solution.py:100
  667.5 6.8 fusion.30
  674.2 7.4 %reshape.72 = bf16[8,64,4096]{2,0,1:T(8,128)(2,1)} reshape(bf16[8,64,8,512]{3,2,0,1:T(8,128)(2,1)} %fusion.30) | data formatting | bytes 8388608 | tf_op jit(solution)/shard_map/reshape | solution.py:106
  681.7 6.5 copy.27
  (97 shorter events, 65.2 us)
Async XLA Ops:
  21.1 209.3 %copy-start = (s32[1,64]{1,0:T(1,128)S(1)}, s32[1,64]{1,0:T(1,128)}, u32[]{:S(2)}) copy-start(s32[1,64]{1,0:T(1,128)} %param.13) | copy-start | bytes 772
  21.1 209.5 %all-to-all-start = ((bf16[8,16,64,512]{3,1,2,0:T(8,128)(2,1)}), bf16[8,16,64,512]{3,1,2,0:T(8,128)(2,1)}, u32[]{:S(2)}, u32[]{:S(2)}) async-start(bf16[8,16,64,512]{3,1,2,0:T(8,128)(2,1)} %copy.23), calls=%async_computation | async-start | bytes 16777216 | tf_op jit(solution)/shard_map/all_to_all | solution.py:51
  394.4 237.9 %all-to-all-start.1 = ((bf16[1,16,512,512]{3,1,0,2:T(8,128)(2,1)}), bf16[1,16,512,512]{3,1,0,2:T(8,128)(2,1)}, u32[]{:S(2)}, u32[]{:S(2)}) async-start(bf16[1,16,512,512]{3,1,0,2:T(8,128)(2,1)} %bitcast.92), calls=%async_computation.1 | async-start | bytes 16777216 | tf_op jit(solution)/shard_map/all_to_all | solution.py:92
where the time goes:
time: 695 us; the launch traced here: 688 us
  blocking collectives  216 us (31%)
  waiting for transfers between devices  171 us (25%)
  local copies, waits for them, and re-layouts  147 us (21%)
  starting transfers between devices  64.5 us (9%)
  matrix products  55.6 us (8%)
  other arithmetic  22.2 us (3%)
  loops' own time  11.1 us (2%)
    psum x1, blocking collectives, per_device(): total_square = lax.psum(jnp.sum(grad_wide * grad_wide), ('dp', 'tensor'))  197 us
    all_to_all x1, waiting for transfers between devices, per_device(): lax.all_to_all(precond[None], 'dp', split_axis=2, concat_axis=0, tiled=True)  171 us
    all_to_all x1, starting transfers between devices, per_device(): lax.all_to_all(precond[None], 'dp', split_axis=2, concat_axis=0, tiled=True)  58.1 us
    squeeze x32, local copies, waits for them, and re-layouts, per_device(): lax.map(process, (arrived, stats_left[0], stats_right[0], root_left[0], r...  41.5 us
    dynamic_update_slice x32, local copies, waits for them, and re-layouts, per_device(): lax.map(process, (arrived, stats_left[0], stats_right[0], root_left[0], r...  37.4 us
    while x2, local copies, waits for them, and re-layouts, per_device(): lax.map(process, (arrived, stats_left[0], stats_right[0], root_left[0], r...  22.7 us
    psum x1, blocking collectives, per_device(): adam_total, precond_total = lax.psum((adam_part, precond_part), 'dp')  18.8 us
    dot_general x7, matrix products, compute(): jnp.dot(applied, root_two, preferred_element_type=jnp.float32)  14.6 us
  transfers between devices with their start and end apart: 2, of which 1 were waited for; matrix products, arithmetic and copies ran while one was open for 2% of the time, Pallas kernels for 0%

commit v1 on v0

v1 whole, which is shorter than its diff:
```python
import functools
import math

import jax
import jax.numpy as jnp
from jax import lax
from jax.experimental import pallas as pl
from jax.experimental.pallas import tpu as pltpu
from jax.sharding import PartitionSpec as P

clip_level = 0.5
decay_moment = 0.95
decay_stats = 0.9
eps_adam = 1e-08
eps_graft = 1e-06
vmem_bytes = 48 * 1024 * 1024


def params():
    return pltpu.CompilerParams(vmem_limit_bytes=vmem_bytes)


def pack_kernel(col_blocks, block_size, count, blocks_ref, grad_ref, out_ref):
    owner = pl.program_id(0)
    for at in range(count):
        block = blocks_ref[owner * count + at]
        row = block // col_blocks
        column = pl.multiple_of((block % col_blocks) * block_size, block_size)
        out_ref[0, at] = grad_ref[row, :, pl.ds(column, block_size)]


def pack(blocks, gradient, owners, block_size):
    count = blocks.shape[0] // owners
    row_blocks, piece_rows, columns = gradient.shape
    return pl.pallas_call(
        functools.partial(pack_kernel, columns // block_size, block_size, count),
        grid_spec=pltpu.PrefetchScalarGridSpec(
            num_scalar_prefetch=1,
            grid=(owners,),
            in_specs=[pl.BlockSpec((row_blocks, piece_rows, columns), lambda o, b: (0, 0, 0))],
            out_specs=pl.BlockSpec((1, count, piece_rows, block_size), lambda o, b: (o, 0, 0, 0)),
        ),
        out_shape=jax.ShapeDtypeStruct((owners, count, piece_rows, block_size), jnp.bfloat16),
        compiler_params=params(),
        name="pack",
    )(blocks, gradient)


def slot_kernel(
    slots_ref, active_ref, clip_ref, grad_ref, left_ref, right_ref, root_left_ref, root_right_ref,
    left_out, right_out, precond_out, norm_out,
):
    at = pl.program_id(0)
    owners, _, piece_rows, block_size = grad_ref.shape

    @pl.when(active_ref[at] != 0)
    def _():
        clip = clip_ref[0]
        factor = (1.0 - decay_stats) * (clip * clip)
        block = grad_ref[...].reshape(block_size, block_size)
        gram_left = lax.dot_general(
            block, block, (((1,), (1,)), ((), ())), preferred_element_type=jnp.float32
        )
        left_out[0, 0] = decay_stats * left_ref[0, 0] + factor * gram_left
        gram_right = lax.dot_general(
            block, block, (((0,), (0,)), ((), ())), preferred_element_type=jnp.float32
        )
        right_out[0, 0] = decay_stats * right_ref[0, 0] + factor * gram_right
        scaled = (clip * block.astype(jnp.float32)).astype(jnp.bfloat16)
        applied = jnp.dot(
            root_left_ref[0, 0], scaled, preferred_element_type=jnp.float32
        ).astype(jnp.bfloat16)
        precond = jnp.dot(
            applied, root_right_ref[0, 0], preferred_element_type=jnp.float32
        ).astype(jnp.bfloat16)
        precond_out[...] = precond.reshape(owners, 1, piece_rows, block_size)
        wide = precond.astype(jnp.float32)
        norm_out[0] = jnp.sum(wide * wide, axis=0, keepdims=True)

    @pl.when(active_ref[at] == 0)
    def _():
        left_out[0, 0] = left_ref[0, 0]
        right_out[0, 0] = right_ref[0, 0]
        precond_out[...] = jnp.zeros_like(precond_out)
        norm_out[...] = jnp.zeros_like(norm_out)


def process_slots(slots, active, clip, arrived, stats_left, stats_right, root_left, root_right):
    owners, capacity, piece_rows, block_size = arrived.shape
    square = pl.BlockSpec((1, 1, block_size, block_size), lambda j, s, a, c: (0, s[j], 0, 0))
    pieces = pl.BlockSpec((owners, 1, piece_rows, block_size), lambda j, s, a, c: (0, j, 0, 0))
    return pl.pallas_call(
        slot_kernel,
        grid_spec=pltpu.PrefetchScalarGridSpec(
            num_scalar_prefetch=3,
            grid=(capacity,),
            in_specs=[pieces, square, square, square, square],
            out_specs=[
                square,
                square,
                pieces,
                pl.BlockSpec((1, 1, block_size), lambda j, s, a, c: (j, 0, 0)),
            ],
        ),
        out_shape=[
            jax.ShapeDtypeStruct(stats_left.shape, jnp.float32),
            jax.ShapeDtypeStruct(stats_right.shape, jnp.float32),
            jax.ShapeDtypeStruct(arrived.shape, jnp.bfloat16),
            jax.ShapeDtypeStruct((capacity, 1, block_size), jnp.float32),
        ],
        compiler_params=params(),
        name="slots",
    )(slots, active, clip, arrived, stats_left, stats_right, root_left, root_right)


def moment_kernel(clip_ref, grad_ref, moment_ref, moment_out, norm_out):
    clipped = clip_ref[0] * grad_ref[0].astype(jnp.float32)
    moment = (
        decay_moment * moment_ref[0].astype(jnp.float32) + (1.0 - decay_moment) * clipped * clipped
    )
    moment_out[0] = moment.astype(jnp.bfloat16)
    adam_step = clipped / (jnp.sqrt(moment) + eps_adam)
    norm_out[0] = jnp.sum(adam_step * adam_step, axis=0, keepdims=True)


def update_moment(clip, gradient, second_moment):
    row_blocks, piece_rows, columns = gradient.shape
    rows = pl.BlockSpec((1, piece_rows, columns), lambda i, c: (i, 0, 0))
    size = gradient.size
    return pl.pallas_call(
        moment_kernel,
        grid_spec=pltpu.PrefetchScalarGridSpec(
            num_scalar_prefetch=1,
            grid=(row_blocks,),
            in_specs=[rows, rows],
            out_specs=[rows, pl.BlockSpec((1, 1, columns), lambda i, c: (i, 0, 0))],
        ),
        out_shape=[
            jax.ShapeDtypeStruct(gradient.shape, jnp.bfloat16),
            jax.ShapeDtypeStruct((row_blocks, 1, columns), jnp.float32),
        ],
        compiler_params=params(),
        cost_estimate=pl.CostEstimate(
            flops=12 * size, bytes_accessed=6 * size, transcendentals=2 * size
        ),
        name="moment",
    )(clip, gradient, second_moment)


def unpack_kernel(col_blocks, places_ref, ratio_ref, *refs):
    out_ref = refs[-1]
    row = pl.program_id(0)
    block_size = out_ref.shape[2] // col_blocks
    for column in range(col_blocks):
        ratio = ratio_ref[row * col_blocks + column]
        wide = refs[column][0, 0].astype(jnp.float32)
        out_ref[0, :, column * block_size : (column + 1) * block_size] = (ratio * wide).astype(
            jnp.bfloat16
        )


def unpack(places, ratio, returned, shape):
    owners, count, piece_rows, block_size = returned.shape
    row_blocks, _, columns = shape
    col_blocks = columns // block_size

    def piece(column):
        def index(i, places, ratio):
            place = places[i * col_blocks + column]
            return (place // count, place % count, 0, 0)

        return pl.BlockSpec((1, 1, piece_rows, block_size), index)

    return pl.pallas_call(
        functools.partial(unpack_kernel, col_blocks),
        grid_spec=pltpu.PrefetchScalarGridSpec(
            num_scalar_prefetch=2,
            grid=(row_blocks,),
            in_specs=[piece(column) for column in range(col_blocks)],
            out_specs=pl.BlockSpec((1, piece_rows, columns), lambda i, p, r: (i, 0, 0)),
        ),
        out_shape=jax.ShapeDtypeStruct(shape, jnp.bfloat16),
        compiler_params=params(),
        name="unpack",
    )(places, ratio, *([returned] * col_blocks))


def per_device(
    gradient, second_moment, slot_of_block, stats_left, stats_right, root_left, root_right
):
    owners = lax.axis_size("dp")
    my_owner = lax.axis_index("dp")
    row_blocks, piece_rows, columns = gradient.shape
    block_size = piece_rows * owners
    col_blocks = columns // block_size
    block_count = row_blocks * col_blocks
    capacity = stats_left.shape[1]
    all_rows = row_blocks * block_size
    all_columns = columns * lax.axis_size("tensor")
    area = float(block_size * block_size)

    table = slot_of_block[0]
    numbers = jnp.arange(block_count, dtype=jnp.int32)
    owner = table // capacity
    ahead = (owner[None, :] == owner[:, None]) & (table[None, :] < table[:, None])
    places = owner * capacity + jnp.sum(ahead, axis=1, dtype=jnp.int32)
    all_places = jnp.arange(owners * capacity, dtype=jnp.int32)
    blocks = jnp.sum(
        jnp.where(places[None, :] == all_places[:, None], numbers[None, :], 0),
        axis=1,
        dtype=jnp.int32,
    )
    local = jnp.arange(capacity, dtype=jnp.int32)
    used = jnp.any(table[None, :] == (my_owner * capacity + local)[:, None], axis=1)
    before = local[None, :] < local[:, None]
    used_count = jnp.sum(used, dtype=jnp.int32)
    order = jnp.where(
        used,
        jnp.sum(before & used[None, :], axis=1, dtype=jnp.int32),
        used_count + jnp.sum(before & ~used[None, :], axis=1, dtype=jnp.int32),
    )
    slots = jnp.sum(
        jnp.where(order[None, :] == local[:, None], local[None, :], 0), axis=1, dtype=jnp.int32
    )
    active = (local < used_count).astype(jnp.int32)

    outgoing = pack(blocks, gradient, owners, block_size)
    arrived = lax.all_to_all(outgoing, "dp", split_axis=0, concat_axis=0, tiled=True)

    grad_wide = gradient.astype(jnp.float32)
    total_square = lax.psum(jnp.sum(grad_wide * grad_wide), ("dp", "tensor"))
    clip_factor = clip_level * math.sqrt(all_rows * all_columns) / jnp.sqrt(total_square)
    clip = clip_factor.reshape(1)

    left_new, right_new, precond, norms = process_slots(
        slots, active, clip, arrived, stats_left, stats_right, root_left, root_right
    )
    returned = lax.all_to_all(precond, "dp", split_axis=0, concat_axis=0, tiled=True)

    later_clip, norms = lax.optimization_barrier((clip, norms))
    moment_new, adam_rows = update_moment(later_clip, gradient, second_moment)
    adam_part = jnp.sum(
        adam_rows.reshape(row_blocks, col_blocks, block_size), axis=2
    ).reshape(block_count)
    owned = places[:, None] == (my_owner * capacity + local)[None, :]
    precond_part = jnp.sum(
        jnp.where(owned, jnp.sum(norms, axis=(1, 2))[None, :], 0.0), axis=1
    )
    adam_total, precond_total = lax.psum((adam_part, precond_part), "dp")
    ratio = jnp.sqrt(adam_total / area / (precond_total / area + eps_graft))
    update = unpack(places, ratio, returned, gradient.shape)
    return update, moment_new, left_new, right_new


def solution(mesh):
    placed = (
        P(None, "dp", "tensor"),
        P(None, "dp", "tensor"),
        P("tensor", None),
        P("tensor", "dp", None, None),
        P("tensor", "dp", None, None),
        P("tensor", "dp", None, None),
        P("tensor", "dp", None, None),
    )
    return jax.shard_map(
        per_device,
        mesh=mesh,
        in_specs=placed,
        out_specs=(
            P(None, "dp", "tensor"),
            P(None, "dp", "tensor"),
            P("tensor", "dp", None, None),
            P("tensor", "dp", None, None),
        ),
        check_vma=False,
    )
```

time: 695 us -> 470 us (0.68)
  waiting for transfers between devices: 171 us -> 0.01 us
  blocking collectives: 216 us -> 374 us
  local copies, waits for them, and re-layouts: 147 us -> 4.45 us
  Pallas kernels: 0 us -> 59.5 us
  matrix products: 55.6 us -> 0 us
  starting transfers between devices: 64.5 us -> 18.1 us
  other arithmetic: 22.2 us -> 11.1 us
  loops' own time: 11.1 us -> 0 us
    all_to_all x2, waiting for transfers between devices: 171 us -> 0.01 us  [the longest x1 0.01 us: per_device(): lax.all_to_all(precond, 'dp', split_axis=0, concat_axis=0, tiled=True)]
    psum x1, blocking collectives: 18.8 us -> 177 us  [per_device(): adam_total, precond_total = lax.psum((adam_part, precond_part), 'dp')]
    pallas_call x0 -> x4, Pallas kernels: none -> 59.5 us  [the longest x1 38.7 us: process_slots(): pl.pallas_call(slot_kernel, grid_spec=pltpu.PrefetchScalarGridSpec(num_sc...]
    dot_general x23 -> x0, matrix products: 55.6 us -> none  [the longest x7 14.6 us: compute(): jnp.dot(applied, root_two, preferred_element_type=jnp.float32)]
    all_to_all x2, starting transfers between devices: 64.5 us -> 18.1 us  [the longest x1 11.7 us: per_device(): lax.all_to_all(precond, 'dp', split_axis=0, concat_axis=0, tiled=True)]
    squeeze x32 -> x0, local copies, waits for them, and re-layouts: 41.5 us -> none  [per_device(): lax.map(process, (arrived, stats_left[0], stats_right[0], root_left[0], r...]
    dynamic_update_slice x32 -> x0, local copies, waits for them, and re-layouts: 37.4 us -> none  [per_device(): lax.map(process, (arrived, stats_left[0], stats_right[0], root_left[0], r...]
    while x2 -> x0, local copies, waits for them, and re-layouts: 22.7 us -> none  [per_device(): lax.map(process, (arrived, stats_left[0], stats_right[0], root_left[0], r...]
  transfers between devices with their start and end apart: 2 -> 2, of which waited for: 1 -> 0; matrix products, arithmetic and copies ran while one was open for 2% -> 2% of each run, Pallas kernels for 0% -> 2%
where the time goes in v1:
time: 470 us; the launch traced here: 468 us
  blocking collectives  374 us (80%)
  Pallas kernels  59.5 us (13%)
  starting transfers between devices  18.1 us (4%)
  other arithmetic  11.1 us (2%)
    psum x1, blocking collectives, per_device(): total_square = lax.psum(jnp.sum(grad_wide * grad_wide), ('dp', 'tensor'))  197 us
    psum x1, blocking collectives, per_device(): adam_total, precond_total = lax.psum((adam_part, precond_part), 'dp')  177 us
    pallas_call x1, Pallas kernels, process_slots(): pl.pallas_call(slot_kernel, grid_spec=pltpu.PrefetchScalarGridSpec(num_sc...  38.7 us
    all_to_all x1, starting transfers between devices, per_device(): lax.all_to_all(precond, 'dp', split_axis=0, concat_axis=0, tiled=True)  11.7 us
  transfers between devices with their start and end apart: 2, of which 0 were waited for; matrix products, arithmetic and copies ran while one was open for 2% of the time, Pallas kernels for 2%

profile of v1, /device:TPU:12, one launch (start us, length us, event | category | flops | bytes accessed | tf_op | source)
XLA Modules:
  0.0 468.3 jit_solution(6997279224528420787)
XLA Ops:
  0.6 0.7 and_select_fusion.1
  1.3 0.7 fusion.4
  2.0 0.9 convert_reduce_fusion
  2.9 0.7 fusion.2
  3.6 0.1 select_reduce_fusion.blocks_ref
  3.6 0.0 copy-start
  3.7 2.2 copy-done
  5.8 5.2 %pack.1 = bf16[8,16,64,512]{3,2,1,0:T(8,128)(2,1)} custom-call(s32[128]{0:T(128)S(1)} %select_reduce_fusion.blocks_ref, bf16[8,64,4096]{2,1,0:T(8,128)(2,1)S(1)} %copy-done), custom_call_target="tpu_custom_call" | custom-call | tf_op jit(solution)/shard_map/pack/pallas_call | solution.py:35
  11.1 0.0 copy-start.2
  11.1 6.4 %all-to-all-start = ((bf16[8,16,64,512]{3,2,1,0:T(8,128)(2,1)}), bf16[8,16,64,512]{3,2,1,0:T(8,128)(2,1)}, u32[]{:S(2)}, u32[]{:S(2)}) async-start(bf16[8,16,64,512]{3,2,1,0:T(8,128)(2,1)} %pack.1), calls=%async_computation | async-start | bytes 16777216 | tf_op jit(solution)/shard_map/all_to_all | solution.py:228
  17.4 4.9 %multiply_reduce_fusion = f32[]{:T(128)} fusion(bf16[8,64,4096]{2,1,0:T(8,128)(2,1)} %grad_ref.3), kind=kLoop, calls=%fused_computation | loop fusion | flops 6291455 | bytes 4194308 | tf_op jit(solution)/shard_map/reduce_sum | solution.py:231
  22.4 197.3 %psum.21 = f32[]{:T(128)} all-reduce(f32[]{:T(128)} %multiply_reduce_fusion), channel_id=1, replica_groups=mesh['dp'=8,'tensor'=4] {'dp','tensor'}, use_global_device_ids=true, to_apply=%region_2.3 | all-reduce | flops 1 | bytes 8 | tf_op jit(solution)/shard_map/psum | solution.py:231
  220.4 0.0 copy-done.2
  220.4 0.2 compare_reduce_fusion
  220.6 0.6 convert_reduce_fusion.3
  221.2 0.6 compare_convert_fusion.active_ref
  221.9 0.1 convert_reduce_fusion.1
  222.0 0.7 add_select_fusion
  222.7 0.1 select_reduce_fusion.2.slots_ref
  222.8 0.0 all-to-all-done.grad_ref
  222.8 38.7 %slots.1 = (f32[1,16,512,512]{3,2,1,0:T(8,128)}, f32[1,16,512,512]{3,2,1,0:T(8,128)}, bf16[8,16,64,512]{3,2,1,0:T(8,128)(2,1)}, f32[16,1,512]{2,1,0:T(1,128)S(1)}) custom-call(s32[16]{0:T(128)S(1)} %select_reduce_fusion.2.slots_ref, s32[16]{0:T(128)S(1)} %compare_convert_fusion.active_ref, f32[1]{0:T(128)} %bitcast.2.clip_ref, ...), custom_call_target="tpu_custom_call" | custom-call | tf_op jit(solution)/shard_map/slots/pallas_call | solution.py:92
  261.5 11.7 %all-to-all-start.1 = ((bf16[8,16,64,512]{3,2,1,0:T(8,128)(2,1)}), bf16[8,16,64,512]{3,2,1,0:T(8,128)(2,1)}, u32[]{:S(2)}, u32[]{:S(2)}) async-start(bf16[8,16,64,512]{3,2,1,0:T(8,128)(2,1)} %get-tuple-element.16), calls=%async_computation.1 | async-start | bytes 16777216 | tf_op jit(solution)/shard_map/all_to_all | solution.py:238
  273.2 0.0 copy-start.1
  273.2 2.2 copy-done.1
  275.4 8.2 %moment.1 = (bf16[8,64,4096]{2,1,0:T(8,128)(2,1)}, f32[8,1,4096]{2,1,0:T(1,128)S(1)}) custom-call(f32[1]{0:T(128)} %bitcast.2.clip_ref, bf16[8,64,4096]{2,1,0:T(8,128)(2,1)S(1)} %copy-done.1, bf16[8,64,4096]{2,1,0:T(8,128)(2,1)} %moment_ref.1), custom_call_target="tpu_custom_call" | custom-call | flops 25165824 | bytes 12582912 | tf_op jit(solution)/shard_map/moment/pallas_call | solution.py:130
  283.6 0.3 reduce
  283.9 0.2 bitcast_reduce_fusion
  284.1 0.1 reshape.84
  284.2 0.2 reduce_sum.101
  284.4 0.1 select_reduce_fusion.1
  284.5 176.5 %all-reduce = (f32[64]{0:T(128)S(1)}, f32[64]{0:T(128)S(1)}) all-reduce(f32[64]{0:T(128)S(1)} %select_reduce_fusion.1, f32[64]{0:T(128)S(1)} %reshape.84), channel_id=1, replica_groups=mesh['dp'=8,'tensor'=4] {'dp'}, use_global_device_ids=true, to_apply=%region_13.14 | all-reduce | flops 128 | bytes 1024 | tf_op jit(solution)/shard_map/psum | solution.py:249
  461.0 0.0 all-to-all-done.1.refs_0_.refs_1_.refs_2_.refs_3_.refs_4_.refs_5_.refs_6_.refs_7_
  461.0 7.3 %unpack.1 = bf16[8,64,4096]{2,1,0:T(8,128)(2,1)} custom-call(s32[64]{0:T(128)S(1)} %multiply_add_fusion.places_ref, f32[64]{0:T(128)S(1)} %fusion.3.ratio_ref, bf16[8,16,64,512]{3,2,1,0:T(8,128)(2,1)} %all-to-all-done.1.refs_0_.refs_1_.refs_2_.refs_3_.refs_4_.refs_5_.refs_6_.refs_7_, ...), custom_call_target="tpu_custom_call" | custom-call | tf_op jit(solution)/shard_map/unpack/pallas_call | solution.py:174
  (4 shorter events, 0.0 us)
Async XLA Ops:
  3.6 2.2 copy-start
  11.1 209.3 %copy-start.2 = (s32[1,64]{1,0:T(1,128)S(1)}, s32[1,64]{1,0:T(1,128)}, u32[]{:S(2)}) copy-start(s32[1,64]{1,0:T(1,128)} %param.9) | copy-start | bytes 772
  11.1 211.7 %all-to-all-start = ((bf16[8,16,64,512]{3,2,1,0:T(8,128)(2,1)}), bf16[8,16,64,512]{3,2,1,0:T(8,128)(2,1)}, u32[]{:S(2)}, u32[]{:S(2)}) async-start(bf16[8,16,64,512]{3,2,1,0:T(8,128)(2,1)} %pack.1), calls=%async_computation | async-start | bytes 16777216 | tf_op jit(solution)/shard_map/all_to_all | solution.py:228
  261.5 199.5 %all-to-all-start.1 = ((bf16[8,16,64,512]{3,2,1,0:T(8,128)(2,1)}), bf16[8,16,64,512]{3,2,1,0:T(8,128)(2,1)}, u32[]{:S(2)}, u32[]{:S(2)}) async-start(bf16[8,16,64,512]{3,2,1,0:T(8,128)(2,1)} %get-tuple-element.16), calls=%async_computation.1 | async-start | bytes 16777216 | tf_op jit(solution)/shard_map/all_to_all | solution.py:238
  273.2 2.2 copy-start.1

commit v2 on v1

--- a/solution.py
+++ b/solution.py
@@ -13,7 +13,7 @@
 decay_stats = 0.9
 eps_adam = 1e-08
 eps_graft = 1e-06
-vmem_bytes = 48 * 1024 * 1024
+vmem_bytes = 60 * 1024 * 1024
 
 
 def params():
@@ -48,8 +48,9 @@
 
 def slot_kernel(
     slots_ref, active_ref, clip_ref, grad_ref, left_ref, right_ref, root_left_ref, root_right_ref,
-    left_out, right_out, precond_out, norm_out,
+    *refs,
 ):
+    left_out, right_out, precond_out, norm_out = refs[-4:]
     at = pl.program_id(0)
     owners, _, piece_rows, block_size = grad_ref.shape
 
@@ -85,16 +86,20 @@
         norm_out[...] = jnp.zeros_like(norm_out)
 
 
-def process_slots(slots, active, clip, arrived, stats_left, stats_right, root_left, root_right):
-    owners, capacity, piece_rows, block_size = arrived.shape
+def process_slots(
+    slots, active, clip, arrived, stats_left, stats_right, root_left, root_right, earlier
+):
+    owners, count, piece_rows, block_size = arrived.shape
     square = pl.BlockSpec((1, 1, block_size, block_size), lambda j, s, a, c: (0, s[j], 0, 0))
     pieces = pl.BlockSpec((owners, 1, piece_rows, block_size), lambda j, s, a, c: (0, j, 0, 0))
+    entries = block_size * block_size
     return pl.pallas_call(
         slot_kernel,
         grid_spec=pltpu.PrefetchScalarGridSpec(
             num_scalar_prefetch=3,
-            grid=(capacity,),
-            in_specs=[pieces, square, square, square, square],
+            grid=(count,),
+            in_specs=[pieces, square, square, square, square]
+            + [pl.BlockSpec(memory_space=pl.ANY)] * len(earlier),
             out_specs=[
                 square,
                 square,
@@ -106,11 +111,17 @@
             jax.ShapeDtypeStruct(stats_left.shape, jnp.float32),
             jax.ShapeDtypeStruct(stats_right.shape, jnp.float32),
             jax.ShapeDtypeStruct(arrived.shape, jnp.bfloat16),
-            jax.ShapeDtypeStruct((capacity, 1, block_size), jnp.float32),
+            jax.ShapeDtypeStruct((count, 1, block_size), jnp.float32),
         ],
+        input_output_aliases={8 + at: at for at in range(len(earlier))},
         compiler_params=params(),
+        cost_estimate=pl.CostEstimate(
+            flops=8 * count * entries * block_size,
+            bytes_accessed=24 * count * entries,
+            transcendentals=0,
+        ),
         name="slots",
-    )(slots, active, clip, arrived, stats_left, stats_right, root_left, root_right)
+    )(slots, active, clip, arrived, stats_left, stats_right, root_left, root_right, *earlier)
 
 
 def moment_kernel(clip_ref, grad_ref, moment_ref, moment_out, norm_out):
@@ -147,42 +158,51 @@
     )(clip, gradient, second_moment)
 
 
-def unpack_kernel(col_blocks, places_ref, ratio_ref, *refs):
+def unpack_kernel(col_blocks, count, parts, places_ref, ratio_ref, *refs):
     out_ref = refs[-1]
     row = pl.program_id(0)
     block_size = out_ref.shape[2] // col_blocks
     for column in range(col_blocks):
-        ratio = ratio_ref[row * col_blocks + column]
-        wide = refs[column][0, 0].astype(jnp.float32)
-        out_ref[0, :, column * block_size : (column + 1) * block_size] = (ratio * wide).astype(
-            jnp.bfloat16
-        )
+        number = row * col_blocks + column
+        ratio = ratio_ref[number]
+        part = (places_ref[number] % (parts * count)) // count
+        for at in range(parts):
+
+            @pl.when(part == at)
+            def _(column=column, at=at, ratio=ratio):
+                wide = refs[column * parts + at][0, 0].astype(jnp.float32)
+                out_ref[0, :, column * block_size : (column + 1) * block_size] = (
+                    ratio * wide
+                ).astype(jnp.bfloat16)
 
 
 def unpack(places, ratio, returned, shape):
-    owners, count, piece_rows, block_size = returned.shape
+    parts = len(returned)
+    owners, count, piece_rows, block_size = returned[0].shape
     row_blocks, _, columns = shape
     col_blocks = columns // block_size
 
-    def piece(column):
+    def piece(column, at):
         def index(i, places, ratio):
             place = places[i * col_blocks + column]
-            return (place // count, place % count, 0, 0)
+            rank = place % (parts * count)
+            here = (rank // count == at).astype(jnp.int32)
+            return (here * (place // (parts * count)), here * (rank % count), 0, 0)
 
         return pl.BlockSpec((1, 1, piece_rows, block_size), index)
 
     return pl.pallas_call(
-        functools.partial(unpack_kernel, col_blocks),
+        functools.partial(unpack_kernel, col_blocks, count, parts),
         grid_spec=pltpu.PrefetchScalarGridSpec(
             num_scalar_prefetch=2,
             grid=(row_blocks,),
-            in_specs=[piece(column) for column in range(col_blocks)],
+            in_specs=[piece(column, at) for column in range(col_blocks) for at in range(parts)],
             out_specs=pl.BlockSpec((1, piece_rows, columns), lambda i, p, r: (i, 0, 0)),
         ),
         out_shape=jax.ShapeDtypeStruct(shape, jnp.bfloat16),
         compiler_params=params(),
         name="unpack",
-    )(places, ratio, *([returned] * col_blocks))
+    )(places, ratio, *(list(returned) * col_blocks))
 
 
 def per_device(
@@ -224,21 +244,44 @@
     )
     active = (local < used_count).astype(jnp.int32)
 
-    outgoing = pack(blocks, gradient, owners, block_size)
-    arrived = lax.all_to_all(outgoing, "dp", split_axis=0, concat_axis=0, tiled=True)
+    parts = 2 if capacity % 2 == 0 else 1
+    count = capacity // parts
+    by_owner = blocks.reshape(owners, capacity)
+
+    def packed(part):
+        chosen = by_owner[:, part * count : (part + 1) * count].reshape(owners * count)
+        return pack(chosen, gradient, owners, block_size)
+
+    def exchange(pieces):
+        return lax.all_to_all(pieces, "dp", split_axis=0, concat_axis=0, tiled=True)
+
+    outgoing = [packed(part) for part in range(parts)]
+    arrived = [exchange(outgoing[0])]
 
     grad_wide = gradient.astype(jnp.float32)
-    total_square = lax.psum(jnp.sum(grad_wide * grad_wide), ("dp", "tensor"))
+    my_square = jnp.sum(grad_wide * grad_wide)
+    *later, my_square = lax.optimization_barrier((*outgoing[1:], my_square))
+    total_square = lax.psum(my_square, ("dp", "tensor"))
+    *later, total_square = lax.optimization_barrier((*later, total_square))
+    arrived.extend(exchange(pieces) for pieces in later)
     clip_factor = clip_level * math.sqrt(all_rows * all_columns) / jnp.sqrt(total_square)
     clip = clip_factor.reshape(1)
 
-    left_new, right_new, precond, norms = process_slots(
-        slots, active, clip, arrived, stats_left, stats_right, root_left, root_right
-    )
-    returned = lax.all_to_all(precond, "dp", split_axis=0, concat_axis=0, tiled=True)
-
-    later_clip, norms = lax.optimization_barrier((clip, norms))
-    moment_new, adam_rows = update_moment(later_clip, gradient, second_moment)
+    earlier, returned, norms = (), [], []
+    for part in range(parts):
+        chosen = slice(part * count, (part + 1) * count)
+        left_new, right_new, precond, norm = process_slots(
+            slots[chosen], active[chosen], clip, arrived[part],
+            stats_left, stats_right, root_left, root_right, earlier,
+        )
+        earlier = (left_new, right_new)
+        if returned:
+            precond, returned[-1] = lax.optimization_barrier((precond, returned[-1]))
+        returned.append(exchange(precond))
+        norms.append(norm)
+    norms = jnp.concatenate(norms)
+
+    moment_new, adam_rows = update_moment(clip, gradient, second_moment)
     adam_part = jnp.sum(
         adam_rows.reshape(row_blocks, col_blocks, block_size), axis=2
     ).reshape(block_count)

time: 470 us -> 444 us (0.945)
  blocking collectives: 374 us -> 190 us
  waiting for transfers between devices: 0.01 us -> 138 us
  Pallas kernels: 59.5 us -> 72 us
  starting transfers between devices: 18.1 us -> 26.9 us
    all_to_all x2 -> x4, waiting for transfers between devices: 0.01 us -> 138 us  [exchange(): return lax.all_to_all(pieces, 'dp', split_axis=0, concat_axis=0, tiled=True)]
    psum x1, blocking collectives: 197 us -> 100 us  [per_device(): total_square = lax.psum(my_square, ('dp', 'tensor'))]
    psum x1, blocking collectives: 177 us -> 89.3 us  [per_device(): adam_total, precond_total = lax.psum((adam_part, precond_part), 'dp')]
    all_to_all x2 -> x4, starting transfers between devices: 18.1 us -> 26.9 us  [exchange(): return lax.all_to_all(pieces, 'dp', split_axis=0, concat_axis=0, tiled=True)]
    pallas_call x1 -> x2, Pallas kernels: 5.22 us -> 12.8 us  [pack(): pl.pallas_call(functools.partial(pack_kernel, columns // block_size, bloc...]
    pallas_call x1 -> x2, Pallas kernels: 38.7 us -> 38.1 us  [process_slots(): pl.pallas_call(slot_kernel, grid_spec=pltpu.PrefetchScalarGridSpec(num_sc...]
  transfers between devices with their start and end apart: 2 -> 4, of which waited for: 0 -> 2; matrix products, arithmetic and copies ran while one was open for 2% -> 3% of each run, Pallas kernels for 2% -> 12%
where the time goes in v2:
time: 444 us; the launch traced here: 443 us
  blocking collectives  190 us (43%)
  waiting for transfers between devices  138 us (31%)
  Pallas kernels  72 us (16%)
  starting transfers between devices  26.9 us (6%)
  other arithmetic  12.5 us (3%)
    all_to_all x4, waiting for transfers between devices, exchange(): return lax.all_to_all(pieces, 'dp', split_axis=0, concat_axis=0, tiled=True)  138 us
    psum x1, blocking collectives, per_device(): total_square = lax.psum(my_square, ('dp', 'tensor'))  100 us
    psum x1, blocking collectives, per_device(): adam_total, precond_total = lax.psum((adam_part, precond_part), 'dp')  89.3 us
    pallas_call x2, Pallas kernels, process_slots(): pl.pallas_call(slot_kernel, grid_spec=pltpu.PrefetchScalarGridSpec(num_sc...  38.1 us
    all_to_all x4, starting transfers between devices, exchange(): return lax.all_to_all(pieces, 'dp', split_axis=0, concat_axis=0, tiled=True)  26.9 us
    pallas_call x2, Pallas kernels, pack(): pl.pallas_call(functools.partial(pack_kernel, columns // block_size, bloc...  12.8 us
    pallas_call x1, Pallas kernels, unpack(): pl.pallas_call(functools.partial(unpack_kernel, col_blocks, count, parts)...  11.8 us
    pallas_call x1, Pallas kernels, update_moment(): pl.pallas_call(moment_kernel, grid_spec=pltpu.PrefetchScalarGridSpec(num_...  9.26 us
  transfers between devices with their start and end apart: 4, of which 2 were waited for; matrix products, arithmetic and copies ran while one was open for 3% of the time, Pallas kernels for 12%

profile of v2, /device:TPU:12, one launch (start us, length us, event | category | flops | bytes accessed | tf_op | source)
XLA Modules:
  0.0 443.0 jit_solution(10685725042916916295)
XLA Ops:
  0.6 0.7 and_select_fusion.1
  1.3 0.7 fusion.7
  2.0 0.9 convert_reduce_fusion
  2.9 0.7 fusion.2
  3.6 0.1 select_reduce_fusion
  3.6 0.1 reshape.91
  3.7 0.1 fusion.4
  3.8 0.6 reshape.96.blocks_ref
  4.4 6.4 %pack.3 = bf16[8,8,64,512]{3,2,1,0:T(8,128)(2,1)} custom-call(s32[64]{0:T(128)} %reshape.96.blocks_ref, bf16[8,64,4096]{2,1,0:T(8,128)(2,1)} %grad_ref.5), custom_call_target="tpu_custom_call" | custom-call | tf_op jit(solution)/shard_map/pack/pallas_call | solution.py:35
  10.8 6.3 %all-to-all-start = ((bf16[8,8,64,512]{3,2,1,0:T(8,128)(2,1)}), bf16[8,8,64,512]{3,2,1,0:T(8,128)(2,1)}, u32[]{:S(2)}, u32[]{:S(2)}) async-start(bf16[8,8,64,512]{3,2,1,0:T(8,128)(2,1)} %pack.3), calls=%async_computation | async-start | bytes 8388608 | tf_op jit(solution)/shard_map/all_to_all | solution.py:256
  17.1 0.6 reshape.92.blocks_ref
  17.6 6.4 %pack.2 = bf16[8,8,64,512]{3,2,1,0:T(8,128)(2,1)} custom-call(s32[64]{0:T(128)} %reshape.92.blocks_ref, bf16[8,64,4096]{2,1,0:T(8,128)(2,1)} %grad_ref.5), custom_call_target="tpu_custom_call" | custom-call | tf_op jit(solution)/shard_map/pack/pallas_call | solution.py:35
  24.0 4.9 %multiply_reduce_fusion = f32[]{:T(128)} fusion(bf16[8,64,4096]{2,1,0:T(8,128)(2,1)} %grad_ref.5), kind=kLoop, calls=%fused_computation | loop fusion | flops 6291455 | bytes 4194308 | tf_op jit(solution)/shard_map/reduce_sum | solution.py:262
  29.0 100.4 %psum.21 = f32[]{:T(128)} all-reduce(f32[]{:T(128)} %multiply_reduce_fusion), channel_id=1, replica_groups=mesh['dp'=8,'tensor'=4] {'dp','tensor'}, use_global_device_ids=true, to_apply=%region_3.4 | all-reduce | flops 1 | bytes 8 | tf_op jit(solution)/shard_map/psum | solution.py:264
  129.4 0.0 copy-start.3
  129.4 0.0 all-to-all-done.grad_ref
  129.4 6.7 %all-to-all-start.1 = ((bf16[8,8,64,512]{3,2,1,0:T(8,128)(2,1)}), bf16[8,8,64,512]{3,2,1,0:T(8,128)(2,1)}, u32[]{:S(2)}, u32[]{:S(2)}) async-start(bf16[8,8,64,512]{3,2,1,0:T(8,128)(2,1)} %pack.2), calls=%async_computation.1 | async-start | bytes 8388608 | tf_op jit(solution)/shard_map/all_to_all | solution.py:256
  136.1 0.0 copy-done.3
  136.1 0.2 compare_reduce_fusion
  137.0 0.6 convert_reduce_fusion.3
  137.6 0.6 compare_convert_fusion
  138.3 0.1 convert_reduce_fusion.1
  138.4 0.7 add_select_fusion
  139.1 0.1 select_reduce_fusion.2
  139.2 0.6 fusion.6
  139.7 0.6 fusion.5
  140.3 20.0 %slots.2 = (f32[1,16,512,512]{3,2,1,0:T(8,128)}, f32[1,16,512,512]{3,2,1,0:T(8,128)}, bf16[8,8,64,512]{3,2,1,0:T(8,128)(2,1)}, f32[8,1,512]{2,1,0:T(1,128)}) custom-call(s32[8]{0:T(128)} %get-tuple-element.42.slots_ref, s32[8]{0:T(128)} %get-tuple-element.40.active_ref, f32[1]{0:T(128)} %bitcast.4.clip_ref, bf16[8,8,64,512]{3,2,1,0:T(8,128)(2,1)} %all-to-all-done.grad_ref, ...), custom_call_target="tpu_custom_call" | custom-call | flops 8589934592 | bytes 50331648 | tf_op jit(solution)/shard_map/slots/pallas_call | solution.py:96
  160.4 65.8 %all-to-all-done.1.grad_ref = bf16[8,8,64,512]{3,2,1,0:T(8,128)(2,1)} async-done(((bf16[8,8,64,512]{3,2,1,0:T(8,128)(2,1)}), bf16[8,8,64,512]{3,2,1,0:T(8,128)(2,1)}, u32[]{:S(2)}, u32[]{:S(2)}) %all-to-all-start.1) | async-done | bytes 4194336 | tf_op jit(solution)/shard_map/all_to_all | solution.py:256
  226.2 7.0 %all-to-all-start.2 = ((bf16[8,8,64,512]{3,2,1,0:T(8,128)(2,1)}), bf16[8,8,64,512]{3,2,1,0:T(8,128)(2,1)}, u32[]{:S(2)}, u32[]{:S(2)}) async-start(bf16[8,8,64,512]{3,2,1,0:T(8,128)(2,1)} %get-tuple-element.30), calls=%async_computation.2 | async-start | bytes 8388608 | tf_op jit(solution)/shard_map/all_to_all | solution.py:256
  233.2 18.1 %slots.3 = (f32[1,16,512,512]{3,2,1,0:T(8,128)}, f32[1,16,512,512]{3,2,1,0:T(8,128)}, bf16[8,8,64,512]{3,2,1,0:T(8,128)(2,1)}, f32[8,1,512]{2,1,0:T(1,128)}) custom-call(s32[8]{0:T(128)} %get-tuple-element.43.slots_ref, s32[8]{0:T(128)} %get-tuple-element.41.active_ref, f32[1]{0:T(128)} %bitcast.4.clip_ref, ...), custom_call_target="tpu_custom_call", output_to_operand_aliasing={{0}: (8, {}), {1}: (9, {})} | custom-call | flops 8589934592 | bytes 50331648 | tf_op jit(solution)/shard_map/slots/pallas_call | solution.py:96
  251.3 72.0 %all-to-all-done.2.refs_0_.refs_2_.refs_4_.refs_6_.refs_8_.refs_10_.refs_12_.refs_14_ = bf16[8,8,64,512]{3,2,1,0:T(8,128)(2,1)} async-done(((bf16[8,8,64,512]{3,2,1,0:T(8,128)(2,1)}), bf16[8,8,64,512]{3,2,1,0:T(8,128)(2,1)}, u32[]{:S(2)}, u32[]{:S(2)}) %all-to-all-start.2) | async-done | bytes 4194336 | tf_op jit(solution)/shard_map/all_to_all | solution.py:256
  323.3 7.0 %all-to-all-start.3 = ((bf16[8,8,64,512]{3,2,1,0:T(8,128)(2,1)}), bf16[8,8,64,512]{3,2,1,0:T(8,128)(2,1)}, u32[]{:S(2)}, u32[]{:S(2)}) async-start(bf16[8,8,64,512]{3,2,1,0:T(8,128)(2,1)} %get-tuple-element.32), calls=%async_computation.3 | async-start | bytes 8388608 | tf_op jit(solution)/shard_map/all_to_all | solution.py:256
  330.3 0.0 copy-start
  330.3 0.0 copy-start.1
  330.3 9.3 %moment.1 = (bf16[8,64,4096]{2,1,0:T(8,128)(2,1)}, f32[8,1,4096]{2,1,0:T(1,128)}) custom-call(f32[1]{0:T(128)} %bitcast.4.clip_ref, bf16[8,64,4096]{2,1,0:T(8,128)(2,1)} %grad_ref.5, bf16[8,64,4096]{2,1,0:T(8,128)(2,1)} %moment_ref.1), custom_call_target="tpu_custom_call" | custom-call | flops 25165824 | bytes 12582912 | tf_op jit(solution)/shard_map/moment/pallas_call | solution.py:141
  339.5 1.2 reduce
  340.8 0.2 bitcast_reduce_fusion
  340.9 0.1 reshape.95
  341.0 0.0 copy-start.2
  341.0 0.0 copy-done
  341.0 0.0 copy-done.1
  341.0 0.2 maximum_reduce_fusion
  341.2 0.1 select_reduce_fusion.1
  341.3 89.3 %all-reduce = (f32[64]{0:T(128)S(1)}, f32[64]{0:T(128)S(1)}) all-reduce(f32[64]{0:T(128)S(1)} %select_reduce_fusion.1, f32[64]{0:T(128)S(1)} %reshape.95), channel_id=1, replica_groups=mesh['dp'=8,'tensor'=4] {'dp'}, use_global_device_ids=true, to_apply=%region_13.14 | all-reduce | flops 128 | bytes 1024 | tf_op jit(solution)/shard_map/psum | solution.py:292
  430.7 0.5 fusion.3.ratio_ref
  431.2 0.0 all-to-all-done.3.refs_1_.refs_3_.refs_5_.refs_7_.refs_9_.refs_11_.refs_13_.refs_15_
  431.2 0.0 copy-done.2
  431.2 11.8 %unpack.1 = bf16[8,64,4096]{2,1,0:T(8,128)(2,1)} custom-call(s32[64]{0:T(128)} %copy-done.2, f32[64]{0:T(128)} %fusion.3.ratio_ref, bf16[8,8,64,512]{3,2,1,0:T(8,128)(2,1)} %all-to-all-done.2.refs_0_.refs_2_.refs_4_.refs_6_.refs_8_.refs_10_.refs_12_.refs_14_, ...), custom_call_target="tpu_custom_call" | custom-call | tf_op jit(solution)/shard_map/unpack/pallas_call | solution.py:194
  (3 shorter events, 0.0 us)
Async XLA Ops:
  10.8 118.6 %all-to-all-start = ((bf16[8,8,64,512]{3,2,1,0:T(8,128)(2,1)}), bf16[8,8,64,512]{3,2,1,0:T(8,128)(2,1)}, u32[]{:S(2)}, u32[]{:S(2)}) async-start(bf16[8,8,64,512]{3,2,1,0:T(8,128)(2,1)} %pack.3), calls=%async_computation | async-start | bytes 8388608 | tf_op jit(solution)/shard_map/all_to_all | solution.py:256
  129.4 6.7 %copy-start.3 = (s32[1,64]{1,0:T(1,128)S(1)}, s32[1,64]{1,0:T(1,128)}, u32[]{:S(2)}) copy-start(s32[1,64]{1,0:T(1,128)} %param.9) | copy-start | bytes 772
  129.4 96.7 %all-to-all-start.1 = ((bf16[8,8,64,512]{3,2,1,0:T(8,128)(2,1)}), bf16[8,8,64,512]{3,2,1,0:T(8,128)(2,1)}, u32[]{:S(2)}, u32[]{:S(2)}) async-start(bf16[8,8,64,512]{3,2,1,0:T(8,128)(2,1)} %pack.2), calls=%async_computation.1 | async-start | bytes 8388608 | tf_op jit(solution)/shard_map/all_to_all | solution.py:256
  226.2 97.1 %all-to-all-start.2 = ((bf16[8,8,64,512]{3,2,1,0:T(8,128)(2,1)}), bf16[8,8,64,512]{3,2,1,0:T(8,128)(2,1)}, u32[]{:S(2)}, u32[]{:S(2)}) async-start(bf16[8,8,64,512]{3,2,1,0:T(8,128)(2,1)} %get-tuple-element.30), calls=%async_computation.2 | async-start | bytes 8388608 | tf_op jit(solution)/shard_map/all_to_all | solution.py:256
  323.3 108.0 %all-to-all-start.3 = ((bf16[8,8,64,512]{3,2,1,0:T(8,128)(2,1)}), bf16[8,8,64,512]{3,2,1,0:T(8,128)(2,1)}, u32[]{:S(2)}, u32[]{:S(2)}) async-start(bf16[8,8,64,512]{3,2,1,0:T(8,128)(2,1)} %get-tuple-element.32), calls=%async_computation.3 | async-start | bytes 8388608 | tf_op jit(solution)/shard_map/all_to_all | solution.py:256
  330.3 10.7 %copy-start = (f32[8,1,512]{2,1,0:T(1,128)S(1)}, f32[8,1,512]{2,1,0:T(1,128)}, u32[]{:S(2)}) copy-start(f32[8,1,512]{2,1,0:T(1,128)} %get-tuple-element.24) | copy-start | bytes 49156
  330.3 10.8 %copy-start.1 = (f32[8,1,512]{2,1,0:T(1,128)S(1)}, f32[8,1,512]{2,1,0:T(1,128)}, u32[]{:S(2)}) copy-start(f32[8,1,512]{2,1,0:T(1,128)} %get-tuple-element.28) | copy-start | bytes 49156
  341.0 90.2 %copy-start.2 = (s32[64]{0:T(128)}, s32[64]{0:T(128)S(1)}, u32[]{:S(2)}) copy-start(s32[64]{0:T(128)S(1)} %multiply_add_fusion.places_ref) | copy-start | bytes 772
